TPU v7x, 256 devices: a whole 4x4x8 slice. The times are simulated.
256 devices in a mesh: subj: 16 (over y, x), slab: 16 (over z, core).
Axes of the slice: x: 4, y: 4, z: 8, core: 2. Of those that a mesh axis runs over, the one named last changes fastest.
Arguments:
- template: float32 [8192, 128], P('slab'), may hold values from -6 to 6
- images: float32 [16, 8192, 128], P('subj', 'slab'), may hold values from -6 to 6
- velocity: float32 [16, 3, 8192, 128], P('subj', None, 'slab'), may hold values from -6 to 6
- stiffness: float32 [8192, 128], P('slab'), may hold values from 0.1 to 1
- send_rows: int32 [16, 16, 16, 32], P('subj', 'slab'), may hold values from 0 to 511, as said below
- ref_slot: int32 [16, 8192, 8], P('subj', 'slab'), may hold values from 0 to 511, as said below
- columns: int32 [16, 8192, 8, 128], P('subj', 'slab'), may hold values from 0 to 127, as said below
- weights: bfloat16 [16, 8192, 8, 128], P('subj', 'slab'), may hold values from 0 to 0.25
Outputs:
- template_out: float32 [8192, 128], P('slab')
- velocity_out: float32 [16, 3, 8192, 128], P('subj', None, 'slab')
Inputs may be any that keep to these rules, and one draw needn't show every extreme that they name: `send_rows`: local rows of the owner slab. `ref_slot`: for each subject and each owner k and destination slab j, the referenced c lie below a count of that pair between 16 and 32; for each subject one destination slab has the count 32 from every owner. columns[s, g, b, x] differs from x by at most 2.
All inputs are finite; a program needn't handle non-finite values.
Results may differ from a plain program's by a relative error of at most 0.0003.
Values sent between devices are 32-bit elements; how exact they have to be, the bound alone decides.
A program may use at most 64 MiB of HBM per device.

v0:
```python
import jax
import jax.numpy as jnp
from jax import lax
from jax.sharding import PartitionSpec as P

YR = 256
SMOOTH = 2
force_step = 1.0
diffusion_dt = 0.16
template_rate = 2.0


def extended(cells, sides, width):
    for axis, dim in sides:
        count = lax.axis_size(axis)
        ends = count - 1
        head = lax.slice_in_dim(cells, 0, width, axis=dim)
        tail = lax.slice_in_dim(cells, cells.shape[dim] - width, cells.shape[dim], axis=dim)
        cells = jnp.concatenate(
            [
                lax.ppermute(tail, axis, [(i, (i + 1) % count) for i in range(ends)]),
                cells,
                lax.ppermute(head, axis, [((i + 1) % count, i) for i in range(ends)]),
            ],
            axis=dim,
        )
    return cells


def smooth_step(field_padded, coef_padded):
    center = field_padded[:, 1:-1]
    coef_center = coef_padded[1:-1]
    field_yx = jnp.pad(center, ((0, 0), (0, 0), (1, 1), (1, 1)))
    coef_yx = jnp.pad(coef_center, ((0, 0), (1, 1), (1, 1)))
    pairs = [
        (field_padded[:, 2:], coef_padded[2:]),
        (field_padded[:, :-2], coef_padded[:-2]),
        (field_yx[:, :, 2:, 1:-1], coef_yx[:, 2:, 1:-1]),
        (field_yx[:, :, :-2, 1:-1], coef_yx[:, :-2, 1:-1]),
        (field_yx[:, :, 1:-1, 2:], coef_yx[:, 1:-1, 2:]),
        (field_yx[:, :, 1:-1, :-2], coef_yx[:, 1:-1, :-2]),
    ]
    summed = jnp.zeros(center.shape, jnp.float32)
    for neighbour, coef_near in pairs:
        face_coef = 0.5 * (coef_center + coef_near)
        summed = summed + face_coef[None] * (neighbour - center)
    return center + diffusion_dt * summed


def read_ahead(values, offset):
    if offset > 0:
        return jnp.concatenate(
            [values[..., offset:], jnp.zeros(values.shape[:-1] + (offset,), values.dtype)], axis=-1
        )
    if offset < 0:
        return jnp.concatenate(
            [jnp.zeros(values.shape[:-1] + (-offset,), values.dtype), values[..., :offset]], axis=-1
        )
    return values


def per_device(template, images, velocity, stiffness, send_rows, ref_slot, columns, weights):
    slabs = lax.axis_size("slab")
    subjects = lax.axis_size("subj")
    capacity = send_rows.shape[3]
    rows = template.shape[0]
    width = template.shape[1]
    planes = rows // YR
    send_one = send_rows[0, 0]
    sending = template[send_one]
    received = lax.all_to_all(sending, "slab", split_axis=0, concat_axis=0, tiled=True)
    flat_rows = received.reshape(slabs * capacity, width)
    slot_one = ref_slot[0]
    offset_one = columns[0] - jnp.arange(width, dtype=jnp.int32)
    picked = flat_rows[slot_one]
    weight_f = weights[0].astype(jnp.float32)
    values = jnp.zeros(picked.shape, jnp.float32)
    for offset in range(-2, 3):
        values = values + jnp.where(offset_one == offset, read_ahead(picked, offset), 0.0)
    warped = jnp.sum(weight_f * values, axis=1)
    mismatch = warped - images[0]
    contrib = weight_f * mismatch[:, None, :]
    placed = jnp.zeros(contrib.shape, jnp.float32)
    for offset in range(-2, 3):
        placed = placed + read_ahead(jnp.where(offset_one == offset, contrib, 0.0), -offset)
    slot_grad = (
        jnp.zeros((slabs * capacity, width), jnp.float32)
        .at[slot_one.reshape(-1)]
        .add(placed.reshape(-1, width))
    )
    slot_grad = slot_grad.reshape(slabs, capacity, width)
    returned = lax.all_to_all(slot_grad, "slab", split_axis=0, concat_axis=0, tiled=True)
    row_grad = (
        jnp.zeros((rows, width), jnp.float32)
        .at[send_one.reshape(-1)]
        .add(returned.reshape(-1, width))
    )
    summed = lax.psum(row_grad, "subj")
    template_out = template - template_rate * summed / subjects
    warped_grid = warped.reshape(planes, YR, width)
    warped_padded = extended(warped_grid, (("slab", 0),), 1)
    warped_yx = jnp.pad(warped_grid, ((0, 0), (1, 1), (1, 1)))
    along_x = 0.5 * (warped_yx[:, 1:-1, 2:] - warped_yx[:, 1:-1, :-2])
    along_y = 0.5 * (warped_yx[:, 2:, 1:-1] - warped_yx[:, :-2, 1:-1])
    along_z = 0.5 * (warped_padded[2:] - warped_padded[:-2])
    slopes = jnp.stack([along_x, along_y, along_z])
    field = (
        velocity[0].reshape(3, planes, YR, width)
        - force_step * mismatch.reshape(planes, YR, width)[None] * slopes
    )
    coef_grid = stiffness.reshape(planes, YR, width)
    coef_padded = extended(coef_grid, (("slab", 0),), 1)
    for repeat in range(SMOOTH):
        field_padded = extended(field, (("slab", 1),), 1)
        field = smooth_step(field_padded, coef_padded)
    velocity_out = field.reshape(3, rows, width)[None]
    return (template_out, velocity_out)


def solution(mesh):
    return jax.shard_map(
        per_device,
        mesh=mesh,
        in_specs=(
            P("slab", None),
            P("subj", "slab", None),
            P("subj", None, "slab", None),
            P("slab", None),
            P("subj", "slab", None, None),
            P("subj", "slab", None),
            P("subj", "slab", None, None),
            P("subj", "slab", None, None),
        ),
        out_specs=(P("slab", None), P("subj", None, "slab", None)),
        check_vma=False,
    )
```

profile of v0, /device:TPU:2, one launch (start us, length us, event | category | flops | bytes accessed | tf_op | source)
XLA Modules:
  0.0 206.6 jit_solution(10799320863399200082)
XLA Ops:
  7.2 0.0 copy-start.5
  7.2 0.0 copy-start.8
  7.2 0.7 compare_select_fusion.2
  7.9 0.1 reshape.168
  8.0 2.6 %gather_fusion = f32[512,128]{1,0:T(8,128)} fusion(f32[512,128]{1,0:T(8,128)} %param.8, s32[1024]{0:T(1024)S(1)} %pad_clamp_fusion), kind=kCustom, calls=%fused_computation | custom fusion | bytes 526336 | tf_op jit(solution)/shard_map/gather | solution.py:70
  10.6 8.6 %all-to-all-start = ((f32[16,32,128]{2,1,0:T(8,128)}), f32[16,32,128]{2,1,0:T(8,128)S(1)}, u32[]{:S(2)}, u32[]{:S(2)}) async-start(f32[16,32,128]{2,1,0:T(8,128)} %bitcast.6), calls=%async_computation | async-start | bytes 524288 | tf_op jit(solution)/shard_map/all_to_all | solution.py:71
  19.2 0.7 slice_bitcast_fusion.3
  19.9 1.3 collective-permute-start.2
  21.2 3.7 %collective-permute-start.4 = (f32[1,256,128]{2,1,0:T(8,128)}, f32[1,256,128]{2,1,0:T(8,128)}, u32[]{:S(2)}, u32[]{:S(2)}) collective-permute-start(f32[1,256,128]{2,1,0:T(8,128)} %get-tuple-element.27), channel_id=1, source_target_pairs={{0,1},{1,2},{2,3},{3,4},{4,5},{5,6},{6,7},{7,8},{8,9},{9,10},{10,1... | collective-permute-start | bytes 393224 | tf_op jit(solution)/shard_map/ppermute | solution.py:21
  24.9 0.1 copy.10
  25.0 0.2 reshape_squeeze.10
  25.3 0.7 reshape_squeeze.9
  25.9 0.1 copy.11
  26.1 0.2 reshape.176
  26.2 4.1 %all-to-all-done = f32[16,32,128]{2,1,0:T(8,128)S(1)} async-done(((f32[16,32,128]{2,1,0:T(8,128)}), f32[16,32,128]{2,1,0:T(8,128)S(1)}, u32[]{:S(2)}, u32[]{:S(2)}) %all-to-all-start) | async-done | bytes 262176 | tf_op jit(solution)/shard_map/all_to_all | solution.py:71
  30.4 10.8 %gather_fusion.1 = f32[4096,128]{1,0:T(8,128)S(1)} fusion(f32[512,128]{1,0:T(8,128)S(1)} %bitcast.66, s32[4096]{0:T(1024)S(1)} %broadcast_clamp_fusion), kind=kCustom, calls=%fused_computation.1 | custom fusion | bytes 4210688 | tf_op jit(solution)/shard_map/gather | solution.py:75
  41.1 0.7 fusion.86
  41.8 0.0 copy-start.1
  41.8 0.0 copy-start.3
  41.8 0.7 fusion.87
  42.5 0.5 copy-done.1
  43.0 0.7 copy-done.3
  43.7 3.9 %fusion = (f32[512,128]{1,0:T(8,128)S(1)}, pred[512,8,128]{2,1,0:T(8,128)(4,1)S(1)}, pred[512,8,128]{2,1,0:T(8,128)(4,1)S(1)}, pred[512,8,128]{2,1,0:T(8,128)(4,...) fusion(f32[512,8,126]{2,1,0:T(8,128)S(1)} %get-tuple-element.13, ...), kind=kLoop, calls=%fused_computation.14 | loop fusion | flops 9371648 | bytes 16416768 | tf_op jit(solution)/shard_map/reduce_sum | solution.py:80
  47.7 0.7 slice_bitcast_fusion.1
  48.4 1.3 collective-permute-start
  49.7 4.1 %collective-permute-start.1 = (f32[1,256,128]{2,1,0:T(8,128)}, f32[1,256,128]{2,1,0:T(8,128)}, u32[]{:S(2)}, u32[]{:S(2)}) collective-permute-start(f32[1,256,128]{2,1,0:T(8,128)} %get-tuple-element.33), channel_id=1, source_target_pairs={{0,1},{1,2},{2,3},{3,4},{4,5},{5,6},{6,7},{7,8},{8,9},{9,10},{10,1... | collective-permute-start | bytes 393224 | tf_op jit(solution)/shard_map/ppermute | solution.py:21
  53.8 0.0 copy-start.2
  53.9 0.2 convert_multiply_fusion
  54.1 0.5 copy-done.2
  54.5 2.6 %slice_select_fusion.2 = (f32[512,8,127]{2,1,0:T(8,128)S(1)}, f32[512,8,127]{2,1,0:T(8,128)}) fusion(f32[512,8,128]{2,1,0:T(8,128)S(1)} %convert_multiply_fusion, pred[512,8,128]{2,1,0:T(8,128)(4,1)S(1)} %get-tuple-element.4, pred[512,8,128]{2,1,0:T(8,128)(4,1)S(1)} %get-tuple-element.6), kind=kLoop, calls=%fused_computation.17 | loop fusion | flops 1040384 | bytes 9363456 | tf_op jit(solution)/shard_map/jit(_where)/select_n | solution.py:85
  57.2 3.2 %slice_select_fusion.3 = (f32[512,8,126]{2,1,0:T(8,128)}, f32[512,8,126]{2,1,0:T(8,128)}) fusion(f32[512,8,128]{2,1,0:T(8,128)S(1)} %convert_multiply_fusion, pred[512,8,128]{2,1,0:T(8,128)(4,1)S(1)} %get-tuple-element.3, pred[512,8,128]{2,1,0:T(8,128)(4,1)S(1)} %get-tuple-element.7), kind=kLoop, calls=%fused_computation.18 | loop fusion | flops 1032192 | bytes 9289728 | tf_op jit(solution)/shard_map/jit(_where)/select_n | solution.py:85
  60.3 23.1 %scatter_custom_fusion = f32[512,128]{1,0:T(8,128)} fusion(s32[4096]{0:T(1024)S(1)} %bitcast.75, f32[512,8,126]{2,1,0:T(8,128)} %get-tuple-element.9, f32[]{:T(128)} %constant.10.clone.1, f32[512,8,127]{2,1,0:T(8,128)} %get-tuple-element.11, pred[512,8,128]{2,1,0:T(8,128)(4,1)} %get-tuple-element.5, f32[512,8,127]{2,1,0:T(8,128)S(1)} %get-tuple-element.10, ...), kind=kCustom, calls=%fused_computation.19 | custom fusion | flops 4194304 | bytes 10487296 | tf_op jit(solution)/shard_map/scatter-add | solution.py:89
  83.4 4.6 %all-to-all-start.1 = ((f32[16,32,128]{2,1,0:T(8,128)}), f32[16,32,128]{2,1,0:T(8,128)}, u32[]{:S(2)}, u32[]{:S(2)}) async-start(f32[16,32,128]{2,1,0:T(8,128)} %bitcast.71), calls=%async_computation.1 | async-start | bytes 524288 | tf_op jit(solution)/shard_map/all_to_all | solution.py:92
  88.1 0.0 all-reduce.14.cloned.1.call-start
  88.1 0.0 collective-permute-done
  88.1 0.0 collective-permute-done.1
  88.1 1.2 fusion.90
  89.3 0.0 copy-done.7
  89.3 0.0 copy-start.10
  89.4 0.0 copy-start.6
  89.4 0.2 fusion.56
  89.5 0.1 fusion.89
  89.6 1.3 collective-permute-start.3
  90.9 4.0 %collective-permute-start.5 = (f32[3,1,256,128]{3,2,1,0:T(8,128)S(1)}, f32[3,1,256,128]{3,2,1,0:T(8,128)}, u32[]{:S(2)}, u32[]{:S(2)}) collective-permute-start(f32[3,1,256,128]{3,2,1,0:T(8,128)S(1)} %get-tuple-element.19), channel_id=1, source_target_pairs={{0,1},{1,2},{2,3},{3,4},{4,5},{5,6},{6,7},{7,8},{8,9},{9,10},{10,1... | collective-permute-start | bytes 1179656 | tf_op jit(solution)/shard_map/ppermute | solution.py:21
  94.9 0.0 copy-done.10
  94.9 0.0 collective-permute-done.2
  94.9 0.0 collective-permute-done.4
  94.9 0.0 copy-done.6
  94.9 1.2 fusion.74
  96.1 3.4 %all-to-all-done.1 = f32[16,32,128]{2,1,0:T(8,128)} async-done(((f32[16,32,128]{2,1,0:T(8,128)}), f32[16,32,128]{2,1,0:T(8,128)}, u32[]{:S(2)}, u32[]{:S(2)}) %all-to-all-start.1) | async-done | bytes 262176 | tf_op jit(solution)/shard_map/all_to_all | solution.py:92
  99.6 3.3 %scatter_custom_fusion.1 = f32[512,128]{1,0:T(8,128)} fusion(s32[512]{0:T(512)S(1)} %bitcast.76, f32[512,128]{1,0:T(8,128)} %bitcast.13, f32[]{:T(128)} %constant.10.clone.1), kind=kCustom, calls=%fused_computation.120 | custom fusion | flops 65536 | bytes 262656 | tf_op jit(solution)/shard_map/scatter-add | solution.py:96
  102.9 0.0 all-reduce.14.cloned.1.call-update
  102.9 0.0 collective-permute-done.3
  102.9 0.0 collective-permute-done.5
  102.9 0.0 copy-start
  102.9 1.8 fusion.25
  104.7 0.1 fusion.88
  104.8 1.3 collective-permute-start.6
  106.1 3.9 %collective-permute-start.7 = (f32[3,1,256,128]{3,2,1,0:T(8,128)S(1)}, f32[3,1,256,128]{3,2,1,0:T(8,128)}, u32[]{:S(2)}, u32[]{:S(2)}) collective-permute-start(f32[3,1,256,128]{3,2,1,0:T(8,128)S(1)} %get-tuple-element.17), channel_id=1, source_target_pairs={{0,1},{1,2},{2,3},{3,4},{4,5},{5,6},{6,7},{7,8},{8,9},{9,10},{10,1... | collective-permute-start | bytes 1179656 | tf_op jit(solution)/shard_map/ppermute | solution.py:21
  110.0 85.3 %all-reduce.14.cloned.1.call-done = f32[512,128]{1,0:T(8,128)} async-done(((f32[512,128]{1,0:T(8,128)}), f32[512,128]{1,0:T(8,128)}) %all-reduce.14.cloned.1.call-update) | async-done | bytes 262160 | tf_op jit(solution)/shard_map/psum | solution.py:98
  195.4 1.7 multiply_subtract_fusion
  197.1 0.0 collective-permute-done.6
  197.1 0.0 collective-permute-done.7
  197.1 2.6 %fusion.39 = f32[3,2,256,128]{3,2,1,0:T(8,128)} fusion(f32[3,2,256,128]{3,2,1,0:T(8,128)S(1)} %fusion.25, f32[3,1,256,128]{3,2,1,0:T(8,128)} %collective-permute-done.7, f32[3,1,256,128]{3,2,1,0:T(8,128)} %collective-permute-done.6, f32[2,256,128]{2,1,0:T(8,128)S(1)} %get-tuple-element.22, f32[2,256,128]{2,1,0:T(8,128)S(1)} %get-tuple-element.25, ...), kind=kLoop, calls=%fused_computation.66 | loop fusion | flops 4128768 | bytes 3932160 | tf_op jit(solution)/shard_map/add | solution.py:47
  (14 shorter events, 0.1 us)
Async XLA Ops:
  7.2 18.1 %copy-start.9 = (s32[1,1,16,32]{3,2,1,0:T(8,128)S(1)}, s32[1,1,16,32]{3,2,1,0:T(8,128)}, u32[]{:S(2)}) copy-start(s32[1,1,16,32]{3,2,1,0:T(8,128)} %param.12) | copy-start | bytes 6148
  7.2 12.0 %copy-start.5 = (f32[512,128]{1,0:T(8,128)S(1)}, f32[512,128]{1,0:T(8,128)}, u32[]{:S(2)}) copy-start(f32[512,128]{1,0:T(8,128)} %param.11) | copy-start | bytes 786436
  7.2 17.7 %copy-start.8 = (s32[1,512,8]{1,2,0:T(8,128)S(1)}, s32[1,512,8]{1,2,0:T(8,128)}, u32[]{:S(2)}) copy-start(s32[1,512,8]{1,2,0:T(8,128)} %param.13) | copy-start | bytes 49156
  10.6 19.8 %all-to-all-start = ((f32[16,32,128]{2,1,0:T(8,128)}), f32[16,32,128]{2,1,0:T(8,128)S(1)}, u32[]{:S(2)}, u32[]{:S(2)}) async-start(f32[16,32,128]{2,1,0:T(8,128)} %bitcast.6), calls=%async_computation | async-start | bytes 524288 | tf_op jit(solution)/shard_map/all_to_all | solution.py:71
  19.9 75.0 %collective-permute-start.2 = (f32[1,256,128]{2,1,0:T(8,128)}, f32[1,256,128]{2,1,0:T(8,128)}, u32[]{:S(2)}, u32[]{:S(2)}) collective-permute-start(f32[1,256,128]{2,1,0:T(8,128)} %get-tuple-element.26), channel_id=1, source_target_pairs={{1,0},{2,1},{3,2},{4,3},{5,4},{6,5},{7,6},{8,7},{9,8},{10,9},{11,1... | collective-permute-start | bytes 393224 | tf_op jit(solution)/shard_map/ppermute | solution.py:23
  21.2 73.7 %collective-permute-start.4 = (f32[1,256,128]{2,1,0:T(8,128)}, f32[1,256,128]{2,1,0:T(8,128)}, u32[]{:S(2)}, u32[]{:S(2)}) collective-permute-start(f32[1,256,128]{2,1,0:T(8,128)} %get-tuple-element.27), channel_id=1, source_target_pairs={{0,1},{1,2},{2,3},{3,4},{4,5},{5,6},{6,7},{7,8},{8,9},{9,10},{10,1... | collective-permute-start | bytes 393224 | tf_op jit(solution)/shard_map/ppermute | solution.py:21
  41.8 1.2 copy-start.1
  41.8 1.9 copy-start.3
  43.7 10.1 %copy-start.4 = (f32[1,512,128]{2,1,0:T(8,128)S(1)}, f32[1,512,128]{2,1,0:T(8,128)}, u32[]{:S(2)}) copy-start(f32[1,512,128]{2,1,0:T(8,128)} %param.9) | copy-start | bytes 786436
  48.4 39.7 %collective-permute-start = (f32[1,256,128]{2,1,0:T(8,128)}, f32[1,256,128]{2,1,0:T(8,128)S(1)}, u32[]{:S(2)}, u32[]{:S(2)}) collective-permute-start(f32[1,256,128]{2,1,0:T(8,128)} %get-tuple-element.32), channel_id=1, source_target_pairs={{1,0},{2,1},{3,2},{4,3},{5,4},{6,5},{7,6},{8,7},{9,8},{10,9},{11,1... | collective-permute-start | bytes 393224 | tf_op jit(solution)/shard_map/ppermute | solution.py:23
  49.7 38.4 %collective-permute-start.1 = (f32[1,256,128]{2,1,0:T(8,128)}, f32[1,256,128]{2,1,0:T(8,128)}, u32[]{:S(2)}, u32[]{:S(2)}) collective-permute-start(f32[1,256,128]{2,1,0:T(8,128)} %get-tuple-element.33), channel_id=1, source_target_pairs={{0,1},{1,2},{2,3},{3,4},{4,5},{5,6},{6,7},{7,8},{8,9},{9,10},{10,1... | collective-permute-start | bytes 393224 | tf_op jit(solution)/shard_map/ppermute | solution.py:21
  53.8 0.7 copy-start.2
  83.4 5.9 %copy-start.7 = (f32[1,3,512,128]{3,2,1,0:T(8,128)S(1)}, f32[1,3,512,128]{3,2,1,0:T(8,128)}, u32[]{:S(2)}) copy-start(f32[1,3,512,128]{3,2,1,0:T(8,128)} %param.10) | copy-start | bytes 2359300
  83.4 16.1 %all-to-all-start.1 = ((f32[16,32,128]{2,1,0:T(8,128)}), f32[16,32,128]{2,1,0:T(8,128)}, u32[]{:S(2)}, u32[]{:S(2)}) async-start(f32[16,32,128]{2,1,0:T(8,128)} %bitcast.71), calls=%async_computation.1 | async-start | bytes 524288 | tf_op jit(solution)/shard_map/all_to_all | solution.py:92
  88.1 107.3 %all-reduce.14.cloned.1.call-start = ((), (), s32[]{:S(2)}) async-start(), calls=%async_computation.2 | async-start | bytes 524288 | tf_op jit(solution)/shard_map/psum | solution.py:98
  89.3 5.6 %copy-start.10 = (s32[512,1]{0,1:T(1,128)S(1)}, s32[512,1]{0,1:T(1,128)}, u32[]{:S(2)}) copy-start(s32[512,1]{0,1:T(1,128)} %reshape_squeeze.9) | copy-start | bytes 6148
  89.4 5.6 %copy-start.6 = (f32[512,128]{1,0:T(8,128)S(1)}, f32[512,128]{1,0:T(8,128)}, u32[]{:S(2)}) copy-start(f32[512,128]{1,0:T(8,128)} %param.11) | copy-start | bytes 786436
  89.6 13.3 %collective-permute-start.3 = (f32[3,1,256,128]{3,2,1,0:T(8,128)S(1)}, f32[3,1,256,128]{3,2,1,0:T(8,128)}, u32[]{:S(2)}, u32[]{:S(2)}) collective-permute-start(f32[3,1,256,128]{3,2,1,0:T(8,128)S(1)} %get-tuple-element.18), channel_id=1, source_target_pairs={{1,0},{2,1},{3,2},{4,3},{5,4},{6,5},{7,6},{8,7},{9,8},{10,9},{11,1... | collective-permute-start | bytes 1179656 | tf_op jit(solution)/shard_map/ppermute | solution.py:23
  90.9 12.0 %collective-permute-start.5 = (f32[3,1,256,128]{3,2,1,0:T(8,128)S(1)}, f32[3,1,256,128]{3,2,1,0:T(8,128)}, u32[]{:S(2)}, u32[]{:S(2)}) collective-permute-start(f32[3,1,256,128]{3,2,1,0:T(8,128)S(1)} %get-tuple-element.19), channel_id=1, source_target_pairs={{0,1},{1,2},{2,3},{3,4},{4,5},{5,6},{6,7},{7,8},{8,9},{9,10},{10,1... | collective-permute-start | bytes 1179656 | tf_op jit(solution)/shard_map/ppermute | solution.py:21
  102.9 92.5 %copy-start = (f32[512,128]{1,0:T(8,128)S(1)}, f32[512,128]{1,0:T(8,128)}, u32[]{:S(2)}) copy-start(f32[512,128]{1,0:T(8,128)} %param.8) | copy-start | bytes 786436
  104.8 92.3 %collective-permute-start.6 = (f32[3,1,256,128]{3,2,1,0:T(8,128)S(1)}, f32[3,1,256,128]{3,2,1,0:T(8,128)}, u32[]{:S(2)}, u32[]{:S(2)}) collective-permute-start(f32[3,1,256,128]{3,2,1,0:T(8,128)S(1)} %get-tuple-element.16), channel_id=1, source_target_pairs={{1,0},{2,1},{3,2},{4,3},{5,4},{6,5},{7,6},{8,7},{9,8},{10,9},{11,1... | collective-permute-start | bytes 1179656 | tf_op jit(solution)/shard_map/ppermute | solution.py:23
  106.1 91.0 %collective-permute-start.7 = (f32[3,1,256,128]{3,2,1,0:T(8,128)S(1)}, f32[3,1,256,128]{3,2,1,0:T(8,128)}, u32[]{:S(2)}, u32[]{:S(2)}) collective-permute-start(f32[3,1,256,128]{3,2,1,0:T(8,128)S(1)} %get-tuple-element.17), channel_id=1, source_target_pairs={{0,1},{1,2},{2,3},{3,4},{4,5},{5,6},{6,7},{7,8},{8,9},{9,10},{10,1... | collective-permute-start | bytes 1179656 | tf_op jit(solution)/shard_map/ppermute | solution.py:21
Sparse Core Ops, SparseCore 0:
  103.0 92.3 all-reduce.13
where the time goes:
time: 207 us
  waiting for transfers between devices  93 us (45%)
  other arithmetic  45.8 us (22%)
  starting transfers between devices  34.1 us (16%)
  local copies, waits for them, and re-layouts  19.3 us (9%)
  between operations  14.3 us (7%)
    psum x1, waiting for transfers between devices, per_device(): summed = lax.psum(row_grad, 'subj')  85.3 us
    scatter-add x1, other arithmetic, per_device(): slot_grad = jnp.zeros((slabs * capacity, width), jnp.float32).at[slot_one...  23.1 us
    ppermute x4, starting transfers between devices, extended(): lax.ppermute(tail, axis, [(i, (i + 1) % count) for i in range(ends)])  15.8 us
    gather x1, local copies, waits for them, and re-layouts, per_device(): picked = flat_rows[slot_one]  10.8 us
    all_to_all x1, starting transfers between devices, per_device(): lax.all_to_all(sending, 'slab', split_axis=0, concat_axis=0, tiled=True)  8.57 us
    select_n x2, other arithmetic, per_device(): jnp.where(offset_one == offset, contrib, 0.0)  5.79 us
    ppermute x4, starting transfers between devices, extended(): lax.ppermute(head, axis, [((i + 1) % count, i) for i in range(ends)])  5.14 us
    all_to_all x1, starting transfers between devices, per_device(): lax.all_to_all(slot_grad, 'slab', split_axis=0, concat_axis=0, tiled=True)  4.6 us
  transfers between devices with their start and end apart: 11, of which 3 were waited for; matrix products, arithmetic and copies ran while one was open for 28% of the time, Pallas kernels for 0%

commit v1 on v0

--- a/solution.py
+++ b/solution.py
@@ -95,7 +95,7 @@
         .at[send_one.reshape(-1)]
         .add(returned.reshape(-1, width))
     )
-    summed = lax.psum(row_grad, "subj")
+    summed = lax.all_gather(row_grad, "subj").sum(axis=0)
     template_out = template - template_rate * summed / subjects
     warped_grid = warped.reshape(planes, YR, width)
     warped_padded = extended(warped_grid, (("slab", 0),), 1)

time: 207 us -> 161 us (0.78)
  waiting for transfers between devices: 93 us -> 47.2 us
  other arithmetic: 45.8 us -> 42.6 us
  starting transfers between devices: 34.1 us -> 37 us
    psum x1 -> x0, waiting for transfers between devices: 85.3 us -> none  [per_device(): summed = lax.psum(row_grad, 'subj')]
    all_gather x0 -> x1, waiting for transfers between devices: none -> 23.1 us  [per_device(): summed = lax.all_gather(row_grad, 'subj').sum(axis=0)]
    all_to_all x1, waiting for transfers between devices: 3.45 us -> 11.2 us  [per_device(): lax.all_to_all(slot_grad, 'slab', split_axis=0, concat_axis=0, tiled=True)]
    all_to_all x1, waiting for transfers between devices: 4.14 us -> 10.5 us  [per_device(): lax.all_to_all(sending, 'slab', split_axis=0, concat_axis=0, tiled=True)]
    ppermute x4, starting transfers between devices: 15.8 us -> 19.6 us  [extended(): lax.ppermute(tail, axis, [(i, (i + 1) % count) for i in range(ends)])]
    reduce_sum x0 -> x1, other arithmetic: none -> 2.44 us  [per_device(): summed = lax.all_gather(row_grad, 'subj').sum(axis=0)]
    ppermute x4, waiting for transfers between devices: 0.01 us -> 2.35 us  [extended(): lax.ppermute(tail, axis, [(i, (i + 1) % count) for i in range(ends)])]
    add x2, other arithmetic: 4.45 us -> 2.17 us  [smooth_step(): return center + diffusion_dt * summed]
  transfers between devices with their start and end apart: 11 -> 11, of which waited for: 3 -> 5; matrix products, arithmetic and copies ran while one was open for 28% -> 3% of each run, Pallas kernels for 0% -> 0%
where the time goes in v1:
time: 161 us; the launch traced here: 159 us
  waiting for transfers between devices  47.2 us (29%)
  other arithmetic  42.6 us (26%)
  starting transfers between devices  37 us (23%)
  local copies, waits for them, and re-layouts  18.3 us (11%)
  between operations  14.4 us (9%)
    all_gather x1, waiting for transfers between devices, per_device(): summed = lax.all_gather(row_grad, 'subj').sum(axis=0)  23.1 us
    scatter-add x1, other arithmetic, per_device(): slot_grad = jnp.zeros((slabs * capacity, width), jnp.float32).at[slot_one...  23.1 us
    ppermute x4, starting transfers between devices, extended(): lax.ppermute(tail, axis, [(i, (i + 1) % count) for i in range(ends)])  19.6 us
    all_to_all x1, waiting for transfers between devices, per_device(): lax.all_to_all(slot_grad, 'slab', split_axis=0, concat_axis=0, tiled=True)  11.2 us
    gather x1, local copies, waits for them, and re-layouts, per_device(): picked = flat_rows[slot_one]  10.8 us
    all_to_all x1, waiting for transfers between devices, per_device(): lax.all_to_all(sending, 'slab', split_axis=0, concat_axis=0, tiled=True)  10.5 us
    all_to_all x1, starting transfers between devices, per_device(): lax.all_to_all(sending, 'slab', split_axis=0, concat_axis=0, tiled=True)  8.57 us
    select_n x2, other arithmetic, per_device(): jnp.where(offset_one == offset, contrib, 0.0)  5.78 us
  transfers between devices with their start and end apart: 11, of which 5 were waited for; matrix products, arithmetic and copies ran while one was open for 3% of the time, Pallas kernels for 0%

profile of v1, /device:TPU:2, one launch (start us, length us, event | category | flops | bytes accessed | tf_op | source)
XLA Modules:
  0.0 159.5 jit_solution(17962527805601046989)
XLA Ops:
  7.2 0.0 copy-start.8
  7.2 0.7 compare_select_fusion.2
  7.9 0.1 reshape.168
  8.0 2.6 %gather_fusion = f32[512,128]{1,0:T(8,128)} fusion(f32[512,128]{1,0:T(8,128)} %param.8, s32[1024]{0:T(1024)S(1)} %pad_clamp_fusion), kind=kCustom, calls=%fused_computation | custom fusion | bytes 526336 | tf_op jit(solution)/shard_map/gather | solution.py:70
  10.6 8.6 %all-to-all-start = ((f32[16,32,128]{2,1,0:T(8,128)}), f32[16,32,128]{2,1,0:T(8,128)S(1)}, u32[]{:S(2)}, u32[]{:S(2)}) async-start(f32[16,32,128]{2,1,0:T(8,128)} %bitcast.6), calls=%async_computation | async-start | bytes 524288 | tf_op jit(solution)/shard_map/all_to_all | solution.py:71
  19.1 0.0 copy-done.8
  19.1 0.1 copy.12
  19.3 0.2 reshape_squeeze.10
  19.5 0.1 copy.13
  19.6 0.2 reshape.176
  19.8 10.5 %all-to-all-done = f32[16,32,128]{2,1,0:T(8,128)S(1)} async-done(((f32[16,32,128]{2,1,0:T(8,128)}), f32[16,32,128]{2,1,0:T(8,128)S(1)}, u32[]{:S(2)}, u32[]{:S(2)}) %all-to-all-start) | async-done | bytes 262176 | tf_op jit(solution)/shard_map/all_to_all | solution.py:71
  30.3 10.8 %gather_fusion.1 = f32[4096,128]{1,0:T(8,128)S(1)} fusion(f32[512,128]{1,0:T(8,128)S(1)} %bitcast.67, s32[4096]{0:T(1024)S(1)} %broadcast_clamp_fusion), kind=kCustom, calls=%fused_computation.1 | custom fusion | bytes 4210688 | tf_op jit(solution)/shard_map/gather | solution.py:75
  41.1 0.7 fusion.86
  41.8 0.0 copy-start.1
  41.8 0.0 copy-start.3
  41.8 0.7 fusion.87
  42.5 0.5 copy-done.1
  43.0 0.7 copy-done.3
  43.7 3.9 %fusion = (f32[512,128]{1,0:T(8,128)S(1)}, pred[512,8,128]{2,1,0:T(8,128)(4,1)S(1)}, pred[512,8,128]{2,1,0:T(8,128)(4,1)S(1)}, pred[512,8,128]{2,1,0:T(8,128)(4,...) fusion(f32[512,8,126]{2,1,0:T(8,128)S(1)} %get-tuple-element.13, ...), kind=kLoop, calls=%fused_computation.14 | loop fusion | flops 9371648 | bytes 16416768 | tf_op jit(solution)/shard_map/reduce_sum | solution.py:80
  47.6 0.0 copy-done.4
  47.7 0.0 copy-start.2
  47.7 0.2 convert_multiply_fusion
  47.9 0.5 copy-done.2
  48.4 2.6 %slice_select_fusion.2 = (f32[512,8,127]{2,1,0:T(8,128)S(1)}, f32[512,8,127]{2,1,0:T(8,128)}) fusion(f32[512,8,128]{2,1,0:T(8,128)S(1)} %convert_multiply_fusion, pred[512,8,128]{2,1,0:T(8,128)(4,1)S(1)} %get-tuple-element.4, pred[512,8,128]{2,1,0:T(8,128)(4,1)S(1)} %get-tuple-element.6), kind=kLoop, calls=%fused_computation.17 | loop fusion | flops 1040384 | bytes 9363456 | tf_op jit(solution)/shard_map/jit(_where)/select_n | solution.py:85
  51.0 3.2 %slice_select_fusion.3 = (f32[512,8,126]{2,1,0:T(8,128)}, f32[512,8,126]{2,1,0:T(8,128)}) fusion(f32[512,8,128]{2,1,0:T(8,128)S(1)} %convert_multiply_fusion, pred[512,8,128]{2,1,0:T(8,128)(4,1)S(1)} %get-tuple-element.3, pred[512,8,128]{2,1,0:T(8,128)(4,1)S(1)} %get-tuple-element.7), kind=kLoop, calls=%fused_computation.18 | loop fusion | flops 1032192 | bytes 9289728 | tf_op jit(solution)/shard_map/jit(_where)/select_n | solution.py:85
  54.2 23.1 %scatter_custom_fusion = f32[512,128]{1,0:T(8,128)} fusion(s32[4096]{0:T(1024)S(1)} %bitcast.78, f32[512,8,126]{2,1,0:T(8,128)} %get-tuple-element.9, f32[]{:T(128)} %constant.10.clone.1, f32[512,8,127]{2,1,0:T(8,128)} %get-tuple-element.11, pred[512,8,128]{2,1,0:T(8,128)(4,1)} %get-tuple-element.5, f32[512,8,127]{2,1,0:T(8,128)S(1)} %get-tuple-element.10, ...), kind=kCustom, calls=%fused_computation.19 | custom fusion | flops 4194304 | bytes 10487296 | tf_op jit(solution)/shard_map/scatter-add | solution.py:89
  77.2 3.7 %all-to-all-start.1 = ((f32[16,32,128]{2,1,0:T(8,128)}), f32[16,32,128]{2,1,0:T(8,128)S(1)}, u32[]{:S(2)}, u32[]{:S(2)}) async-start(f32[16,32,128]{2,1,0:T(8,128)} %bitcast.73), calls=%async_computation.1 | async-start | bytes 524288 | tf_op jit(solution)/shard_map/all_to_all | solution.py:92
  80.9 0.0 all-gather.3.cloned.1.call-start
  81.0 0.0 copy-done.9
  81.0 0.1 reshape_squeeze.9
  81.1 11.2 %all-to-all-done.1 = f32[16,32,128]{2,1,0:T(8,128)S(1)} async-done(((f32[16,32,128]{2,1,0:T(8,128)}), f32[16,32,128]{2,1,0:T(8,128)S(1)}, u32[]{:S(2)}, u32[]{:S(2)}) %all-to-all-start.1) | async-done | bytes 262176 | tf_op jit(solution)/shard_map/all_to_all | solution.py:92
  92.2 2.9 %scatter_custom_fusion.1 = f32[512,128]{1,0:T(8,128)} fusion(s32[512]{0:T(512)S(1)} %bitcast.79, f32[512,128]{1,0:T(8,128)S(1)} %bitcast.77, f32[]{:T(128)} %constant.10.clone.1), kind=kCustom, calls=%fused_computation.120 | custom fusion | flops 65536 | bytes 262148 | tf_op jit(solution)/shard_map/scatter-add | solution.py:96
  95.2 0.0 all-gather.3.cloned.1.call-update
  95.2 1.3 collective-permute-start
  96.5 3.2 %collective-permute-start.1 = (f32[1,256,128]{2,1,0:T(8,128)S(1)}, f32[1,256,128]{2,1,0:T(8,128)S(1)}, u32[]{:S(2)}, u32[]{:S(2)}) collective-permute-start(f32[1,256,128]{2,1,0:T(8,128)S(1)} %get-tuple-element.33), channel_id=1, source_target_pairs={{0,1},{1,2},{2,3},{3,4},{4,5},{5,6},{6,7},{7,8},{8,9},{9,10},{10,1... | collective-permute-start | bytes 393224 | tf_op jit(solution)/shard_map/ppermute | solution.py:21
  99.7 1.0 slice_bitcast_fusion.3
  100.7 1.3 collective-permute-start.2
  102.0 4.5 %collective-permute-start.4 = (f32[1,256,128]{2,1,0:T(8,128)S(1)}, f32[1,256,128]{2,1,0:T(8,128)S(1)}, u32[]{:S(2)}, u32[]{:S(2)}) collective-permute-start(f32[1,256,128]{2,1,0:T(8,128)S(1)} %get-tuple-element.27), channel_id=1, source_target_pairs={{0,1},{1,2},{2,3},{3,4},{4,5},{5,6},{6,7},{7,8},{8,9},{9,10},{10,1... | collective-permute-start | bytes 393224 | tf_op jit(solution)/shard_map/ppermute | solution.py:21
  106.4 0.0 collective-permute-done
  106.5 0.0 collective-permute-done.1
  106.5 0.0 copy-done.5
  106.5 0.2 fusion.90
  106.7 0.0 copy-done.7
  106.7 0.0 copy-start.6
  106.7 0.2 fusion.56
  106.9 0.1 fusion.89
  106.9 1.3 collective-permute-start.3
  108.2 4.3 %collective-permute-start.5 = (f32[3,1,256,128]{3,2,1,0:T(8,128)S(1)}, f32[3,1,256,128]{3,2,1,0:T(8,128)S(1)}, u32[]{:S(2)}, u32[]{:S(2)}) collective-permute-start(f32[3,1,256,128]{3,2,1,0:T(8,128)S(1)} %get-tuple-element.19), channel_id=1, source_target_pairs={{0,1},{1,2},{2,3},{3,4},{4,5},{5,6},{6,7},{7,8},{8,9},{9,10},{10,1... | collective-permute-start | bytes 1179656 | tf_op jit(solution)/shard_map/ppermute | solution.py:21
  112.5 0.0 collective-permute-done.2
  112.5 0.0 collective-permute-done.4
  112.6 0.0 copy-done.6
  112.6 0.2 fusion.74
  112.8 0.0 collective-permute-done.3
  112.8 1.0 collective-permute-done.5
  113.8 0.6 fusion.25
  114.5 0.1 fusion.88
  114.6 1.3 collective-permute-start.6
  115.9 7.7 %collective-permute-start.7 = (f32[3,1,256,128]{3,2,1,0:T(8,128)S(1)}, f32[3,1,256,128]{3,2,1,0:T(8,128)S(1)}, u32[]{:S(2)}, u32[]{:S(2)}) collective-permute-start(f32[3,1,256,128]{3,2,1,0:T(8,128)S(1)} %get-tuple-element.17), channel_id=1, source_target_pairs={{0,1},{1,2},{2,3},{3,4},{4,5},{5,6},{6,7},{7,8},{8,9},{9,10},{10,1... | collective-permute-start | bytes 1179656 | tf_op jit(solution)/shard_map/ppermute | solution.py:21
  123.5 0.0 collective-permute-done.6
  123.5 1.3 collective-permute-done.7
  124.8 1.5 fusion.39
  126.4 23.1 %all-gather.3.cloned.1.call-done = f32[8192,128]{1,0:T(8,128)} async-done(((f32[512,128]{1,0:T(8,128)}), f32[8192,128]{1,0:T(8,128)}) %all-gather.3.cloned.1.call-update) | async-done | bytes 4194320 | tf_op jit(solution)/shard_map/all_gather | solution.py:98
  149.5 2.4 %reduce_sum.21 = f32[512,128]{1,0:T(8,128)S(1)} reduce(f32[16,512,128]{2,1,0:T(8,128)} %bitcast.71, f32[]{:T(128)} %constant.10.clone.1), dimensions={0}, to_apply=%region_3.4 | reduce | flops 983040 | bytes 4456452 | tf_op jit(solution)/shard_map/reduce_sum | solution.py:98
  151.9 0.7 multiply_subtract_fusion
  (13 shorter events, 0.1 us)
Async XLA Ops:
  7.2 12.0 %copy-start.8 = (s32[1,512,8]{1,2,0:T(8,128)S(1)}, s32[1,512,8]{1,2,0:T(8,128)}, u32[]{:S(2)}) copy-start(s32[1,512,8]{1,2,0:T(8,128)} %param.13) | copy-start | bytes 49156
  10.6 19.8 %all-to-all-start = ((f32[16,32,128]{2,1,0:T(8,128)}), f32[16,32,128]{2,1,0:T(8,128)S(1)}, u32[]{:S(2)}, u32[]{:S(2)}) async-start(f32[16,32,128]{2,1,0:T(8,128)} %bitcast.6), calls=%async_computation | async-start | bytes 524288 | tf_op jit(solution)/shard_map/all_to_all | solution.py:71
  41.8 1.2 copy-start.1
  41.8 1.9 %copy-start.3 = (s32[1,512,8,128]{3,2,1,0:T(8,128)S(1)}, s32[1,512,8,128]{3,2,1,0:T(8,128)}, u32[]{:S(2)}) copy-start(s32[1,512,8,128]{3,2,1,0:T(8,128)} %param.14) | copy-start | bytes 6291460
  43.7 3.9 %copy-start.4 = (f32[1,512,128]{2,1,0:T(8,128)S(1)}, f32[1,512,128]{2,1,0:T(8,128)}, u32[]{:S(2)}) copy-start(f32[1,512,128]{2,1,0:T(8,128)} %param.9) | copy-start | bytes 786436
  47.7 0.7 copy-start.2
  54.2 26.8 %copy-start.9 = (s32[1,1,16,32]{3,2,1,0:T(8,128)S(1)}, s32[1,1,16,32]{3,2,1,0:T(8,128)}, u32[]{:S(2)}) copy-start(s32[1,1,16,32]{3,2,1,0:T(8,128)} %param.12) | copy-start | bytes 6148
  77.2 29.2 %copy-start.5 = (f32[1,512,128]{2,1,0:T(8,128)S(1)}, f32[1,512,128]{2,1,0:T(8,128)}, u32[]{:S(2)}) copy-start(f32[1,512,128]{2,1,0:T(8,128)} %param.9) | copy-start | bytes 786436
  77.2 29.5 %copy-start.7 = (f32[1,3,512,128]{3,2,1,0:T(8,128)S(1)}, f32[1,3,512,128]{3,2,1,0:T(8,128)}, u32[]{:S(2)}) copy-start(f32[1,3,512,128]{3,2,1,0:T(8,128)} %param.10) | copy-start | bytes 2359300
  77.2 15.0 %all-to-all-start.1 = ((f32[16,32,128]{2,1,0:T(8,128)}), f32[16,32,128]{2,1,0:T(8,128)S(1)}, u32[]{:S(2)}, u32[]{:S(2)}) async-start(f32[16,32,128]{2,1,0:T(8,128)} %bitcast.73), calls=%async_computation.1 | async-start | bytes 524288 | tf_op jit(solution)/shard_map/all_to_all | solution.py:92
  80.9 68.5 %all-gather.3.cloned.1.call-start = ((), (), s32[]{:S(2)}) async-start(), calls=%async_computation.2 | async-start | bytes 4456448 | tf_op jit(solution)/shard_map/all_gather | solution.py:98
  95.2 11.2 %collective-permute-start = (f32[1,256,128]{2,1,0:T(8,128)S(1)}, f32[1,256,128]{2,1,0:T(8,128)S(1)}, u32[]{:S(2)}, u32[]{:S(2)}) collective-permute-start(f32[1,256,128]{2,1,0:T(8,128)S(1)} %get-tuple-element.32), channel_id=1, source_target_pairs={{1,0},{2,1},{3,2},{4,3},{5,4},{6,5},{7,6},{8,7},{9,8},{10,9},{11,1... | collective-permute-start | bytes 393224 | tf_op jit(solution)/shard_map/ppermute | solution.py:23
  96.5 9.9 %collective-permute-start.1 = (f32[1,256,128]{2,1,0:T(8,128)S(1)}, f32[1,256,128]{2,1,0:T(8,128)S(1)}, u32[]{:S(2)}, u32[]{:S(2)}) collective-permute-start(f32[1,256,128]{2,1,0:T(8,128)S(1)} %get-tuple-element.33), channel_id=1, source_target_pairs={{0,1},{1,2},{2,3},{3,4},{4,5},{5,6},{6,7},{7,8},{8,9},{9,10},{10,1... | collective-permute-start | bytes 393224 | tf_op jit(solution)/shard_map/ppermute | solution.py:21
  100.7 11.8 %collective-permute-start.2 = (f32[1,256,128]{2,1,0:T(8,128)S(1)}, f32[1,256,128]{2,1,0:T(8,128)S(1)}, u32[]{:S(2)}, u32[]{:S(2)}) collective-permute-start(f32[1,256,128]{2,1,0:T(8,128)S(1)} %get-tuple-element.26), channel_id=1, source_target_pairs={{1,0},{2,1},{3,2},{4,3},{5,4},{6,5},{7,6},{8,7},{9,8},{10,9},{11,1... | collective-permute-start | bytes 393224 | tf_op jit(solution)/shard_map/ppermute | solution.py:23
  102.0 10.6 %collective-permute-start.4 = (f32[1,256,128]{2,1,0:T(8,128)S(1)}, f32[1,256,128]{2,1,0:T(8,128)S(1)}, u32[]{:S(2)}, u32[]{:S(2)}) collective-permute-start(f32[1,256,128]{2,1,0:T(8,128)S(1)} %get-tuple-element.27), channel_id=1, source_target_pairs={{0,1},{1,2},{2,3},{3,4},{4,5},{5,6},{6,7},{7,8},{8,9},{9,10},{10,1... | collective-permute-start | bytes 393224 | tf_op jit(solution)/shard_map/ppermute | solution.py:21
  106.7 5.8 %copy-start.6 = (f32[512,128]{1,0:T(8,128)S(1)}, f32[512,128]{1,0:T(8,128)}, u32[]{:S(2)}) copy-start(f32[512,128]{1,0:T(8,128)} %param.11) | copy-start | bytes 786436
  106.9 5.8 %collective-permute-start.3 = (f32[3,1,256,128]{3,2,1,0:T(8,128)S(1)}, f32[3,1,256,128]{3,2,1,0:T(8,128)S(1)}, u32[]{:S(2)}, u32[]{:S(2)}) collective-permute-start(f32[3,1,256,128]{3,2,1,0:T(8,128)S(1)} %get-tuple-element.18), channel_id=1, source_target_pairs={{1,0},{2,1},{3,2},{4,3},{5,4},{6,5},{7,6},{8,7},{9,8},{10,9},{11,1... | collective-permute-start | bytes 1179656 | tf_op jit(solution)/shard_map/ppermute | solution.py:23
  108.2 5.6 %collective-permute-start.5 = (f32[3,1,256,128]{3,2,1,0:T(8,128)S(1)}, f32[3,1,256,128]{3,2,1,0:T(8,128)S(1)}, u32[]{:S(2)}, u32[]{:S(2)}) collective-permute-start(f32[3,1,256,128]{3,2,1,0:T(8,128)S(1)} %get-tuple-element.19), channel_id=1, source_target_pairs={{0,1},{1,2},{2,3},{3,4},{4,5},{5,6},{6,7},{7,8},{8,9},{9,10},{10,1... | collective-permute-start | bytes 1179656 | tf_op jit(solution)/shard_map/ppermute | solution.py:21
  114.6 9.0 %collective-permute-start.6 = (f32[3,1,256,128]{3,2,1,0:T(8,128)S(1)}, f32[3,1,256,128]{3,2,1,0:T(8,128)S(1)}, u32[]{:S(2)}, u32[]{:S(2)}) collective-permute-start(f32[3,1,256,128]{3,2,1,0:T(8,128)S(1)} %get-tuple-element.16), channel_id=1, source_target_pairs={{1,0},{2,1},{3,2},{4,3},{5,4},{6,5},{7,6},{8,7},{9,8},{10,9},{11,1... | collective-permute-start | bytes 1179656 | tf_op jit(solution)/shard_map/ppermute | solution.py:23
  115.9 9.0 %collective-permute-start.7 = (f32[3,1,256,128]{3,2,1,0:T(8,128)S(1)}, f32[3,1,256,128]{3,2,1,0:T(8,128)S(1)}, u32[]{:S(2)}, u32[]{:S(2)}) collective-permute-start(f32[3,1,256,128]{3,2,1,0:T(8,128)S(1)} %get-tuple-element.17), channel_id=1, source_target_pairs={{0,1},{1,2},{2,3},{3,4},{4,5},{5,6},{6,7},{7,8},{8,9},{9,10},{10,1... | collective-permute-start | bytes 1179656 | tf_op jit(solution)/shard_map/ppermute | solution.py:21
  149.5 2.5 %copy-start = (f32[512,128]{1,0:T(8,128)S(1)}, f32[512,128]{1,0:T(8,128)}, u32[]{:S(2)}) copy-start(f32[512,128]{1,0:T(8,128)} %param.8) | copy-start | bytes 786436
Sparse Core Ops, SparseCore 0:
  95.3 54.1 all-gather.2
